TPU v7x, 32 devices: a whole 2x2x4 slice. The times are simulated.
32 devices in a mesh: dp: 4 (over y, core), expert: 8 (over z, x).
Axes of the slice: x: 2, y: 2, z: 4, core: 2. Of those that a mesh axis runs over, the one named last changes fastest.
Arguments:
- tokens: bfloat16 [4096, 2048], P(('dp', 'expert')), may hold values from -6 to 6
- tangents: bfloat16 [4096, 2048], P(('dp', 'expert')), may hold values from -6 to 6
- cotangents: bfloat16 [4096, 2048], P(('dp', 'expert')), may hold values from -6 to 6
- routes: int32 [4096, 2], P(('dp', 'expert')), may hold values from 0 to 7, all different within a row; in each aligned block of 128 rows (0 to 127, 128 to 255, ...) at most 64 rows name the same one
- gates: bfloat16 [4096, 2], P(('dp', 'expert')), may hold values from 0.19921875 to 1
- w_up: bfloat16 [8, 2048, 768], P('expert'), may hold values from -0.125 to 0.125
- w_down: bfloat16 [8, 768, 2048], P('expert'), may hold values from -0.21875 to 0.21875
- v_up: bfloat16 [8, 2048, 768], P('expert'), may hold values from -0.125 to 0.125
Outputs:
- hvp_tokens: bfloat16 [4096, 2048], P(('dp', 'expert'))
- hvp_up: bfloat16 [8, 2048, 768], P('expert', 'dp')
- hvp_down: bfloat16 [8, 768, 2048], P('expert', None, 'dp')
Inputs may be any that keep to these rules, and one draw needn't show every extreme that they name: `routes`: A token's 2 experts differ. Among the 128 tokens of one device no expert is named more than 64 times, and in every draw some device names some expert exactly 64 times.
All inputs are finite; a program needn't handle non-finite values.
Results may differ from a plain program's by a relative error of at most 0.014.
Values may be sent and summed in bfloat16 or wider, within the bound.
A program may use at most 128 MiB of HBM per device.

v0:
```python
import math

import jax
import jax.numpy as jnp
from jax import lax
from jax.sharding import PartitionSpec as P


def slot_table(route_ids, expert_count, capacity):
    token_count, route_count = route_ids.shape
    flat_ids = route_ids.reshape(token_count * route_count)
    onehot = (flat_ids[:, None] == jnp.arange(expert_count, dtype=jnp.int32)[None, :]).astype(
        jnp.int32
    )
    before = jnp.cumsum(onehot, axis=0) - onehot
    slot_rank = jnp.sum(before * onehot, axis=1)
    target = flat_ids * capacity + slot_rank
    slot_owner = (
        jnp.full((expert_count * capacity,), -1, jnp.int32)
        .at[target]
        .set(jnp.arange(token_count * route_count, dtype=jnp.int32))
    )
    return (target, slot_owner)


def gather_slots(rows, slot_owner, route_count):
    valid = slot_owner >= 0
    safe = jnp.where(valid, slot_owner, 0) // route_count
    picked = jnp.take(rows, safe, axis=0)
    return jnp.where(valid[:, None], picked, jnp.zeros_like(picked))


def gather_gates(gate_rows, slot_owner):
    valid = slot_owner >= 0
    flat_gate = gate_rows.reshape(-1)
    picked = jnp.take(flat_gate, jnp.where(valid, slot_owner, 0), axis=0)
    return jnp.where(valid, picked, jnp.zeros_like(picked))


def per_device(tokens, tangents, cotangents, routes, gates, w_up, w_down, v_up):
    token_count, width = tokens.shape
    route_count = routes.shape[1]
    expert_count = lax.axis_size("expert")
    replicas = lax.axis_size("dp")
    capacity = max(2, token_count * route_count * 2 // expert_count)
    scale = 1.0 / math.sqrt(token_count * route_count * replicas)
    target, slot_owner = slot_table(routes, expert_count, capacity)
    send_primal = gather_slots(tokens, slot_owner, route_count).reshape(
        expert_count, capacity, width
    )
    send_tangent = gather_slots(tangents, slot_owner, route_count).reshape(
        expert_count, capacity, width
    )
    send_cotan = gather_slots(cotangents, slot_owner, route_count).reshape(
        expert_count, capacity, width
    )
    send_gate = gather_gates(gates, slot_owner).reshape(expert_count, capacity)
    primal = lax.all_to_all(send_primal, "expert", split_axis=0, concat_axis=0, tiled=True)
    tangent = lax.all_to_all(send_tangent, "expert", split_axis=0, concat_axis=0, tiled=True)
    cotan, gate_slot = (
        lax.all_to_all(send_cotan, "expert", split_axis=0, concat_axis=0, tiled=True),
        lax.all_to_all(send_gate, "expert", split_axis=0, concat_axis=0, tiled=True),
    )
    slots = expert_count * capacity
    primal = primal.reshape(slots, width)
    tangent = tangent.reshape(slots, width)
    cotan = cotan.reshape(slots, width)
    gate_slot = gate_slot.reshape(slots)
    up_proj = w_up[0]
    down_proj = w_down[0]
    dir_up = v_up[0]
    pre_act = jnp.dot(primal, up_proj, preferred_element_type=jnp.float32)
    pre_tan = jnp.dot(tangent, up_proj, preferred_element_type=jnp.float32) + jnp.dot(
        primal, dir_up, preferred_element_type=jnp.float32
    )
    sigmoid_z = jax.nn.sigmoid(pre_act)
    first_der = sigmoid_z * (1.0 + pre_act * (1.0 - sigmoid_z))
    second_der = sigmoid_z * (1.0 - sigmoid_z) * (2.0 + pre_act * (1.0 - 2.0 * sigmoid_z))
    hidden_tan = (first_der * pre_tan).astype(jnp.bfloat16)
    scaled_cot = (gate_slot.astype(jnp.float32)[:, None] * cotan.astype(jnp.float32)).astype(
        jnp.bfloat16
    )
    back_hid = jnp.dot(scaled_cot, down_proj.T, preferred_element_type=jnp.float32)
    back_pre = (back_hid * first_der).astype(jnp.bfloat16)
    back_tan = (back_hid * second_der * pre_tan).astype(jnp.bfloat16)
    input_hvp = (
        jnp.dot(back_tan, up_proj.T, preferred_element_type=jnp.float32)
        + jnp.dot(back_pre, dir_up.T, preferred_element_type=jnp.float32)
    ).astype(jnp.bfloat16)
    returned = lax.all_to_all(
        input_hvp.reshape(expert_count, capacity, width),
        "expert",
        split_axis=0,
        concat_axis=0,
        tiled=True,
    )
    route_rows = jnp.take(returned.reshape(slots, width), target, axis=0).astype(jnp.float32)
    hvp_tokens = jnp.sum(route_rows.reshape(token_count, route_count, width), axis=1).astype(
        jnp.bfloat16
    )
    first = jnp.dot(tangent.T, back_pre, preferred_element_type=jnp.float32) + jnp.dot(
        primal.T, back_tan, preferred_element_type=jnp.float32
    )
    second = jnp.dot(scaled_cot.T, hidden_tan, preferred_element_type=jnp.float32)
    summed = lax.psum_scatter(
        (jnp.concatenate([first, second], axis=1) * scale).astype(jnp.bfloat16),
        "dp",
        scatter_dimension=0,
        tiled=True,
    ).astype(jnp.float32)
    hidden_units = up_proj.shape[1]
    hvp_up = summed[:, :hidden_units].astype(jnp.bfloat16)[None]
    hvp_down = summed[:, hidden_units:].T.astype(jnp.bfloat16)[None]
    return (hvp_tokens, hvp_up, hvp_down)


def solution(mesh):
    in_specs = (
        P(("dp", "expert"), None),
        P(("dp", "expert"), None),
        P(("dp", "expert"), None),
        P(("dp", "expert"), None),
        P(("dp", "expert"), None),
        P("expert", None, None),
        P("expert", None, None),
        P("expert", None, None),
    )
    out_specs = (P(("dp", "expert"), None), P("expert", "dp", None), P("expert", None, "dp"))
    return jax.shard_map(
        per_device, mesh=mesh, in_specs=in_specs, out_specs=out_specs, check_vma=False
    )
```

profile of v0, /device:TPU:0, one launch (start us, length us, event | category | flops | bytes accessed | tf_op | source)
XLA Modules:
  0.0 317.7 jit_solution(6227256782868084722)
XLA Ops:
  7.2 0.8 broadcast_multiply_fusion
  8.0 0.9 copy.29
  10.4 1.4 scatter_custom_fusion
  12.8 3.4 %gather_fusion = bf16[512]{0:T(512)(128)(2,1)S(1)} fusion(bf16[256]{0:T(256)(128)(2,1)S(1)} %reshape.130, s32[1024]{0:T(1024)S(1)} %pad_clamp_fusion.2), kind=kCustom, calls=%fused_computation.3 | custom fusion | bytes 4096 | tf_op jit(solution)/shard_map/jit(_take)/gather | solution.py:36
  16.9 7.3 %all-to-all-start = ((bf16[8,1,64]{2,1,0:T(2,128)(2,1)}), bf16[8,1,64]{2,1,0:T(2,128)(2,1)S(1)}, u32[]{:S(2)}, u32[]{:S(2)}) async-start(bf16[8,1,64]{2,1,0:T(2,128)(2,1)} %all_to_all.24), calls=%async_computation | async-start | bytes 8192 | tf_op jit(solution)/shard_map/all_to_all | solution.py:62
  24.1 6.4 %gather_fusion.4 = bf16[512,2048]{1,0:T(8,128)(2,1)} fusion(bf16[128,2048]{1,0:T(8,128)(2,1)} %param.11, s32[1024]{0:T(1024)S(1)} %pad_clamp_fusion.1), kind=kCustom, calls=%fused_computation.2.clone | custom fusion | bytes 4196352 | tf_op jit(solution)/shard_map/jit(_take)/gather | solution.py:29
  30.5 6.3 %gather_fusion.3 = bf16[512,2048]{1,0:T(8,128)(2,1)} fusion(bf16[128,2048]{1,0:T(8,128)(2,1)} %param.10, s32[1024]{0:T(1024)S(1)} %pad_clamp_fusion.1), kind=kCustom, calls=%fused_computation.1.clone | custom fusion | bytes 4196352 | tf_op jit(solution)/shard_map/jit(_take)/gather | solution.py:29
  36.9 6.4 %gather_fusion.2 = bf16[512,2048]{1,0:T(8,128)(2,1)} fusion(bf16[128,2048]{1,0:T(8,128)(2,1)} %param.12, s32[1024]{0:T(1024)S(1)} %pad_clamp_fusion.1), kind=kCustom, calls=%fused_computation.clone | custom fusion | bytes 4196352 | tf_op jit(solution)/shard_map/jit(_take)/gather | solution.py:29
  43.2 4.8 %select_select_fusion = (bf16[512,2048]{1,0:T(8,128)(2,1)}, bf16[512,2048]{1,0:T(8,128)(2,1)}, bf16[512,2048]{1,0:T(8,128)(2,1)}) fusion(bf16[512,2048]{1,0:T(8,128)(2,1)} %gather_fusion.4, pred[512]{0:T(512)(128)(4,1)S(1)} %get-tuple-element.19, pred[512]{0:T(512)(128)(4,1)S(1)} %get-tuple-element.21, bf16[512,2048]{1,0:T(8,128)(2,1)} %gather_fusion.3, ...), kind=kLoop, calls=%fused_computation.27 | loop fusion | flops 6291456 | bytes 12583936 | tf_op jit(solution)/shard_map/jit(_where)/select_n | solution.py:30
  48.0 54.0 %all_to_all.30 = bf16[8,64,2048]{2,1,0:T(8,128)(2,1)} all-to-all(bf16[8,64,2048]{2,1,0:T(8,128)(2,1)} %bitcast.66), channel_id=1, replica_groups=mesh['dp'=4,'expert'=8] {'expert'}, dimensions={0} | all-to-all | bytes 4194304 | tf_op jit(solution)/shard_map/all_to_all | solution.py:61
  102.1 51.2 %all_to_all.31 = bf16[8,64,2048]{2,1,0:T(8,128)(2,1)} all-to-all(bf16[8,64,2048]{2,1,0:T(8,128)(2,1)S(1)} %bitcast.65), channel_id=1, replica_groups=mesh['dp'=4,'expert'=8] {'expert'}, dimensions={0} | all-to-all | bytes 4194304 | tf_op jit(solution)/shard_map/all_to_all | solution.py:58
  153.3 4.3 %all-to-all-start.3 = ((bf16[8,64,2048]{2,1,0:T(8,128)(2,1)}), bf16[8,64,2048]{2,1,0:T(8,128)(2,1)}, u32[]{:S(2)}, u32[]{:S(2)}) async-start(bf16[8,64,2048]{2,1,0:T(8,128)(2,1)} %bitcast.64), calls=%async_computation.3 | async-start | bytes 4194304 | tf_op jit(solution)/shard_map/all_to_all | solution.py:59
  158.0 4.8 %fusion.10 = f32[512,768]{1,0:T(8,128)} fusion(bf16[512,2048]{1,0:T(8,128)(2,1)} %bitcast.61, bf16[1,2048,768]{2,1,0:T(8,128)(2,1)S(1)} %copy-done), kind=kOutput, calls=%fused_computation.21 | convolution fusion | flops 1610612736 | bytes 6815744 | tf_op jit(solution)/shard_map/dot_general | solution.py:72
  162.8 3.0 fusion.4
  166.2 1.5 copy-done.10
  167.7 3.0 fusion.12
  170.7 34.2 %all-to-all-done.3 = bf16[8,64,2048]{2,1,0:T(8,128)(2,1)} async-done(((bf16[8,64,2048]{2,1,0:T(8,128)(2,1)}), bf16[8,64,2048]{2,1,0:T(8,128)(2,1)}, u32[]{:S(2)}, u32[]{:S(2)}) %all-to-all-start.3) | async-done | bytes 2097184 | tf_op jit(solution)/shard_map/all_to_all | solution.py:59
  204.9 5.3 %fusion.19 = (bf16[512,768]{1,0:T(8,128)(2,1)S(1)}, bf16[512,768]{1,0:T(8,128)(2,1)S(1)}, f32[512,768]{1,0:T(8,128)S(1)}) fusion(f32[512,768]{1,0:T(8,128)} %fusion.12, f32[512,768]{1,0:T(8,128)} %fusion.10, f32[512,768]{1,0:T(8,128)} %fusion.4, bf16[512,2048]{1,0:T(8,128)(2,1)} %bitcast.12, bf16[1,2048,768]{2,1,0:T(8,128)(2,1)S(1)} %copy-done), kind=kOutput, calls=%fused_computation.34 | convolution fusion | flops 1618083840 | bytes 13107200 | tf_op jit(solution)/shard_map/dot_general | solution.py:73
  210.3 4.0 %fusion.36 = f32[2048,768]{0,1:T(8,128)S(1)} fusion(bf16[512,2048]{1,0:T(8,128)(2,1)} %bitcast.12, bf16[512,768]{1,0:T(8,128)(2,1)S(1)} %get-tuple-element.23), kind=kOutput, calls=%fused_computation.75 | convolution fusion | flops 1610612736 | bytes 9175040 | tf_op jit(solution)/shard_map/dot_general | solution.py:101
  214.7 1.0 copy-done.12
  215.7 4.7 %fusion.26 = f32[2048,768]{0,1:T(8,128)} fusion(bf16[512,2048]{1,0:T(8,128)(2,1)S(1)} %fusion.1, f32[512,768]{1,0:T(8,128)S(1)} %get-tuple-element.29, f32[512,768]{1,0:T(8,128)S(1)} %copy-done.12), kind=kOutput, calls=%fused_computation.42 | convolution fusion | flops 1614151680 | bytes 11534336 | tf_op jit(solution)/shard_map/dot_general | solution.py:104
  220.5 4.7 %convolution_add_fusion = f32[2048,768]{0,1:T(8,128)} fusion(f32[2048,768]{0,1:T(8,128)S(1)} %fusion.36, bf16[512,2048]{1,0:T(8,128)(2,1)S(1)} %bitcast.63, bf16[512,768]{1,0:T(8,128)(2,1)S(1)} %get-tuple-element.22), kind=kOutput, calls=%fused_computation.12 | convolution fusion | flops 1612185600 | bytes 15466496 | tf_op jit(solution)/shard_map/dot_general | solution.py:101
  225.2 9.1 %fusion = bf16[2048,1536]{0,1:T(8,128)(2,1)} fusion(f32[2048,768]{0,1:T(8,128)} %fusion.26, f32[2048,768]{0,1:T(8,128)} %convolution_add_fusion), kind=kLoop, calls=%fused_computation.7 | loop fusion | flops 9437184 | bytes 18874368 | tf_op jit(solution)/shard_map/convert_element_type | solution.py:106
  234.2 4.0 %fusion.2 = f32[512,2048]{1,0:T(8,128)S(1)} fusion(bf16[512,768]{1,0:T(8,128)(2,1)} %copy-done.8, bf16[1,2048,768]{2,1,0:T(8,128)(2,1)} %param.17), kind=kOutput, calls=%fused_computation.13 | convolution fusion | flops 1610612736 | bytes 8126464 | tf_op jit(solution)/shard_map/dot_general | solution.py:88
  238.3 3.2 %add_convert_fusion = bf16[512,2048]{1,0:T(8,128)(2,1)} fusion(f32[512,2048]{1,0:T(8,128)S(1)} %fusion.2, bf16[512,768]{1,0:T(8,128)(2,1)S(1)} %copy-done.7, bf16[1,2048,768]{2,1,0:T(8,128)(2,1)S(1)} %copy-done), kind=kOutput, calls=%fused_computation.10 | convolution fusion | flops 1612709888 | bytes 10223616 | tf_op jit(solution)/shard_map/dot_general | solution.py:87
  241.5 4.6 %all-to-all-start.4 = ((bf16[8,64,2048]{2,1,0:T(8,128)(2,1)}), bf16[8,64,2048]{2,1,0:T(8,128)(2,1)}, u32[]{:S(2)}, u32[]{:S(2)}) async-start(bf16[8,64,2048]{2,1,0:T(8,128)(2,1)} %bitcast.68), calls=%async_computation.4 | async-start | bytes 4194304 | tf_op jit(solution)/shard_map/all_to_all | solution.py:90
  246.5 47.3 %all-to-all-done.4 = bf16[8,64,2048]{2,1,0:T(8,128)(2,1)} async-done(((bf16[8,64,2048]{2,1,0:T(8,128)(2,1)}), bf16[8,64,2048]{2,1,0:T(8,128)(2,1)}, u32[]{:S(2)}, u32[]{:S(2)}) %all-to-all-start.4) | async-done | bytes 2097184 | tf_op jit(solution)/shard_map/all_to_all | solution.py:90
  293.8 5.3 %gather_fusion.1 = bf16[256,2048]{1,0:T(8,128)(2,1)} fusion(bf16[512,2048]{1,0:T(8,128)(2,1)} %bitcast.15, s32[1024]{0:T(1024)S(1)} %pad_clamp_fusion), kind=kCustom, calls=%fused_computation.4 | custom fusion | bytes 2098176 | tf_op jit(solution)/shard_map/jit(_take)/gather | solution.py:97
  299.0 2.5 gather.15
  301.6 4.4 %fusion.25 = bf16[128,2048]{1,0:T(8,128)(2,1)} fusion(bf16[128,2,2048]{2,1,0:T(2,128)(2,1)} %gather.15, pred[128,2]{1,0:T(8,128)(4,1)S(1)} %copy.32), kind=kLoop, calls=%fused_computation.41 | loop fusion | flops 786432 | bytes 1573120 | tf_op jit(solution)/shard_map/reduce_sum | solution.py:98
  305.9 2.6 slice_bitcast_fusion
  308.6 2.3 copy.36
  (58 shorter events, 4.7 us)
Async XLA Ops:
  7.2 150.8 %copy-start = (bf16[1,2048,768]{2,1,0:T(8,128)(2,1)S(1)}, bf16[1,2048,768]{2,1,0:T(8,128)(2,1)}, u32[]{:S(2)}) copy-start(bf16[1,2048,768]{2,1,0:T(8,128)(2,1)} %param.15) | copy-start | bytes 9437188
  16.9 31.2 %all-to-all-start = ((bf16[8,1,64]{2,1,0:T(2,128)(2,1)}), bf16[8,1,64]{2,1,0:T(2,128)(2,1)S(1)}, u32[]{:S(2)}, u32[]{:S(2)}) async-start(bf16[8,1,64]{2,1,0:T(2,128)(2,1)} %all_to_all.24), calls=%async_computation | async-start | bytes 8192 | tf_op jit(solution)/shard_map/all_to_all | solution.py:62
  48.0 54.0 %copy-start.5 = (bf16[512,2048]{1,0:T(8,128)(2,1)S(1)}, bf16[512,2048]{1,0:T(8,128)(2,1)}, u32[]{:S(2)}) copy-start(bf16[512,2048]{1,0:T(8,128)(2,1)} %get-tuple-element.27) | copy-start | bytes 6291460
  153.3 51.6 %all-to-all-start.3 = ((bf16[8,64,2048]{2,1,0:T(8,128)(2,1)}), bf16[8,64,2048]{2,1,0:T(8,128)(2,1)}, u32[]{:S(2)}, u32[]{:S(2)}) async-start(bf16[8,64,2048]{2,1,0:T(8,128)(2,1)} %bitcast.64), calls=%async_computation.3 | async-start | bytes 4194304 | tf_op jit(solution)/shard_map/all_to_all | solution.py:59
  157.6 148.3 %reduce-scatter.2.cloned.1.call-start = ((), (), s32[]{:S(2)}) async-start(), calls=%async_computation.6 | async-start | bytes 7864320 | tf_op jit(solution)/shard_map/reduce_scatter | solution.py:105
  158.0 4.8 %copy-start.3 = (bf16[8,64,2048]{2,1,0:T(8,128)(2,1)S(1)}, bf16[8,64,2048]{2,1,0:T(8,128)(2,1)}, u32[]{:S(2)}) copy-start(bf16[8,64,2048]{2,1,0:T(8,128)(2,1)} %all_to_all.31) | copy-start | bytes 6291460
  158.0 4.8 %copy-start.11 = (bf16[1,2048,768]{2,1,0:T(8,128)(2,1)S(1)}, bf16[1,2048,768]{2,1,0:T(8,128)(2,1)}, u32[]{:S(2)}) copy-start(bf16[1,2048,768]{2,1,0:T(8,128)(2,1)} %param.17) | copy-start | bytes 9437188
  162.8 3.0 copy-start.1
  165.8 1.9 copy-start.10
  210.2 4.1 %copy-start.8 = (bf16[512,768]{1,0:T(8,128)(2,1)}, bf16[512,768]{1,0:T(8,128)(2,1)S(1)}, u32[]{:S(2)}) copy-start(bf16[512,768]{1,0:T(8,128)(2,1)S(1)} %get-tuple-element.23) | copy-start | bytes 2359300
  210.2 10.2 %copy-start.6 = (bf16[512,768]{1,0:T(8,128)(2,1)}, bf16[512,768]{1,0:T(8,128)(2,1)S(1)}, u32[]{:S(2)}) copy-start(bf16[512,768]{1,0:T(8,128)(2,1)S(1)} %get-tuple-element.22) | copy-start | bytes 2359300
  210.2 4.1 %copy-start.2 = (bf16[8,64,2048]{2,1,0:T(8,128)(2,1)S(1)}, bf16[8,64,2048]{2,1,0:T(8,128)(2,1)}, u32[]{:S(2)}) copy-start(bf16[8,64,2048]{2,1,0:T(8,128)(2,1)} %all_to_all.30) | copy-start | bytes 6291460
  214.3 1.4 copy-start.12
  215.7 4.7 %copy-start.4 = (bf16[8,64,2048]{2,1,0:T(8,128)(2,1)S(1)}, bf16[8,64,2048]{2,1,0:T(8,128)(2,1)}, u32[]{:S(2)}) copy-start(bf16[8,64,2048]{2,1,0:T(8,128)(2,1)} %all_to_all.31) | copy-start | bytes 6291460
  234.2 4.0 %copy-start.7 = (bf16[512,768]{1,0:T(8,128)(2,1)S(1)}, bf16[512,768]{1,0:T(8,128)(2,1)}, u32[]{:S(2)}) copy-start(bf16[512,768]{1,0:T(8,128)(2,1)} %copy-done.6) | copy-start | bytes 2359300
  241.5 4.8 %copy-start.9 = (s32[128,2]{0,1:T(2,128)S(1)}, s32[128,2]{0,1:T(2,128)}, u32[]{:S(2)}) copy-start(s32[128,2]{0,1:T(2,128)} %param.13) | copy-start | bytes 3076
  241.5 52.3 %all-to-all-start.4 = ((bf16[8,64,2048]{2,1,0:T(8,128)(2,1)}), bf16[8,64,2048]{2,1,0:T(8,128)(2,1)}, u32[]{:S(2)}, u32[]{:S(2)}) async-start(bf16[8,64,2048]{2,1,0:T(8,128)(2,1)} %bitcast.68), calls=%async_computation.4 | async-start | bytes 4194304 | tf_op jit(solution)/shard_map/all_to_all | solution.py:90
Sparse Core Ops, SparseCore 0:
  234.4 57.4 reduce-scatter.1
where the time goes:
time: 319 us; the launch traced here: 318 us
  blocking collectives  105 us (33%)
  waiting for transfers between devices  81.5 us (26%)
  local copies, waits for them, and re-layouts  42.7 us (13%)
  matrix products  36.8 us (12%)
  other arithmetic  20.7 us (6%)
  starting transfers between devices  16.4 us (5%)
  between operations  14.3 us (4%)
    all_to_all x1, blocking collectives, per_device(): lax.all_to_all(send_cotan, 'expert', split_axis=0, concat_axis=0, tiled=T...  54 us
    all_to_all x1, blocking collectives, per_device(): lax.all_to_all(send_primal, 'expert', split_axis=0, concat_axis=0, tiled=...  51.2 us
    all_to_all x1, waiting for transfers between devices, per_device(): lax.all_to_all(input_hvp.reshape(expert_count, capacity, width), 'expert'...  47.3 us
    all_to_all x1, waiting for transfers between devices, per_device(): lax.all_to_all(send_tangent, 'expert', split_axis=0, concat_axis=0, tiled...  34.2 us
    gather x3, local copies, waits for them, and re-layouts, gather_slots(): picked = jnp.take(rows, safe, axis=0)  19.1 us
    convert_element_type x1, other arithmetic, per_device(): (jnp.concatenate([first, second], axis=1) * scale).astype(jnp.bfloat16)  9.05 us
    gather x2, local copies, waits for them, and re-layouts, per_device(): jnp.take(returned.reshape(slots, width), target, axis=0).astype(jnp.float32)  7.79 us
    all_to_all x1, starting transfers between devices, per_device(): lax.all_to_all(send_gate, 'expert', split_axis=0, concat_axis=0, tiled=True)  7.25 us
  transfers between devices with their start and end apart: 4, of which 2 were waited for; matrix products, arithmetic and copies ran while one was open for 17% of the time, Pallas kernels for 0%

commit v1 on v0

v1 whole, which is shorter than its diff:
```python
import functools
import math

import jax
import jax.numpy as jnp
from jax import lax
from jax.experimental import pallas as pl
from jax.experimental.pallas import tpu as pltpu
from jax.sharding import PartitionSpec as P

MESH = pl.DeviceIdType.MESH
F32 = jnp.float32
BF16 = jnp.bfloat16


def route_rows(routes, gates, expert_count):
    token_count = routes.shape[0]
    hit = routes[:, :, None] == jnp.arange(expert_count, dtype=jnp.int32)[None, None, :]
    mask = jnp.any(hit, axis=1)
    rank = jnp.cumsum(mask.astype(jnp.int32), axis=0) - 1
    slot = jnp.where(mask, rank, -1).astype(F32)
    gate = jnp.sum(jnp.where(hit, gates.astype(F32)[:, :, None], 0.0), axis=1)
    return jnp.concatenate([slot.T, gate.T], axis=0).reshape(2 * expert_count, token_count)


def layer_kernel(
    n, inner, cap,
    meta, tok, tan, cot, w_up, w_down, v_up,
    out, rows, hid,
    mbuf, gbuf, sbuf, hback, hsend, pbuf, psend, wu, wd, vu,
    load_sem, own_send, fwd_send, g_recv, x_send, x_recv, h_send, h_recv, p_send, p_recv,
):
    me = lax.axis_index("expert")
    z = me // inner
    x = me % inner
    experts = n * inner
    tokens = gbuf.shape[2]

    def at(outer_pos, inner_pos):
        return {"expert": outer_pos * inner + inner_pos}

    def peer(o):
        return lax.rem(x + o, inner)

    own = [
        pltpu.make_async_copy(src, dst, load_sem.at[i])
        for i, (src, dst) in enumerate(
            [
                (meta, mbuf.at[z]),
                (tok, gbuf.at[0, z]),
                (tan, gbuf.at[1, z]),
                (cot, gbuf.at[2, z]),
                (w_up, wu),
                (v_up, vu),
                (w_down, wd),
            ]
        )
    ]
    for c in own:
        c.start()

    barrier = pltpu.get_barrier_semaphore()
    has_left = z > 0
    has_right = z < n - 1
    for cond, pos in ((has_left, z - 1), (has_right, z + 1)):

        @pl.when(cond)
        def _():
            pl.semaphore_signal(barrier, inc=1, device_id=at(pos, x), device_id_type=MESH)

    for o in range(1, inner):
        pl.semaphore_signal(barrier, inc=1, device_id=at(z, peer(o)), device_id_type=MESH)
    for o in range(1, n):
        far = lax.rem(z + o, n)

        @pl.when(jnp.logical_and(far != z - 1, far != z + 1))
        def _():
            pl.semaphore_signal(barrier, inc=1, device_id=at(far, x), device_id_type=MESH)

    pl.semaphore_wait(barrier, n - 1 + inner - 1)

    def block(a, j):
        return mbuf.at[j] if a == 0 else gbuf.at[a - 1, j]

    def hop(a, j, pos, send_sem):
        return pltpu.make_async_remote_copy(
            src_ref=block(a, j),
            dst_ref=block(a, j),
            send_sem=send_sem,
            recv_sem=g_recv.at[a, j],
            device_id=at(pos, x),
            device_id_type=MESH,
        )

    for a in range(4):
        own[a].wait()

        @pl.when(has_left)
        def _():
            hop(a, z, z - 1, own_send.at[a, 0]).start()

        @pl.when(has_right)
        def _():
            hop(a, z, z + 1, own_send.at[a, 1]).start()

    near = jnp.minimum(z, n - 1 - z)
    left_half = z < n - 1 - z

    def source(k):
        d = (k + 1) // 2
        toward = jnp.where(left_half, d, -d)
        close = jnp.where(k % 2 == 1, z + toward, z - toward)
        return jnp.where(k <= 2 * near, close, jnp.where(left_half, k, n - 1 - k))

    def picks(j):
        slots = lax.broadcasted_iota(jnp.int32, (cap, tokens), 0).astype(F32)
        ones, gated = [], []
        for o in range(inner):
            e = z * inner + peer(o)
            hit = mbuf[j, pl.ds(e, 1), :] == slots
            ones.append(jnp.where(hit, 1.0, 0.0))
            gated.append(jnp.where(hit, mbuf[j, pl.ds(experts + e, 1), :], 0.0))
        return jnp.concatenate(ones, axis=0), jnp.concatenate(gated, axis=0)

    def x_copy(a, j, o):
        return pltpu.make_async_remote_copy(
            src_ref=sbuf.at[j, a, o - 1],
            dst_ref=rows.at[j, a, pl.ds((inner - o) * cap, cap)],
            send_sem=x_send.at[a, j, o - 1],
            recv_sem=x_recv.at[a, j, inner - o - 1],
            device_id=at(z, peer(o)),
            device_id_type=MESH,
        )

    def x_arrival(a, j, o):
        return pltpu.make_async_remote_copy(
            src_ref=sbuf.at[j, a, o - 1],
            dst_ref=rows.at[j, a, pl.ds(o * cap, cap)],
            send_sem=x_send.at[a, j, o - 1],
            recv_sem=x_recv.at[a, j, o - 1],
            device_id=at(z, peer(o)),
            device_id_type=MESH,
        )

    def h_copy(j, o):
        return pltpu.make_async_remote_copy(
            src_ref=hsend.at[j, o - 1],
            dst_ref=hback.at[j, pl.ds((inner - o) * cap, cap)],
            send_sem=h_send.at[j, o - 1],
            recv_sem=h_recv.at[j, inner - o - 1],
            device_id=at(z, peer(o)),
            device_id_type=MESH,
        )

    def h_arrival(j, o):
        return pltpu.make_async_remote_copy(
            src_ref=hsend.at[j, o - 1],
            dst_ref=hback.at[j, pl.ds(o * cap, cap)],
            send_sem=h_send.at[j, o - 1],
            recv_sem=h_recv.at[j, o - 1],
            device_id=at(z, peer(o)),
            device_id_type=MESH,
        )

    def p_copy(j):
        return pltpu.make_async_remote_copy(
            src_ref=psend.at[j],
            dst_ref=pbuf.at[z],
            send_sem=p_send.at[j],
            recv_sem=p_recv.at[z],
            device_id=at(j, x),
            device_id_type=MESH,
        )

    def p_arrival(j):
        return pltpu.make_async_remote_copy(
            src_ref=psend.at[j],
            dst_ref=pbuf.at[j],
            send_sem=p_send.at[j],
            recv_sem=p_recv.at[j],
            device_id=at(j, x),
            device_id_type=MESH,
        )

    def bring(k):
        j = source(k)
        forward_left = jnp.logical_and(j > z, has_left)
        forward_right = jnp.logical_and(j < z, has_right)

        def take(a):
            @pl.when(j != z)
            def _():
                hop(a, j, z, fwd_send.at[a, j]).wait_recv()

                @pl.when(forward_left)
                def _():
                    hop(a, j, z - 1, fwd_send.at[a, j]).start()

                @pl.when(forward_right)
                def _():
                    hop(a, j, z + 1, fwd_send.at[a, j]).start()

        take(0)
        ones, gated = picks(j)
        for a in range(3):
            take(a + 1)
            pick = (gated if a == 2 else ones).astype(BF16)
            got = jnp.dot(pick, gbuf[a, j], preferred_element_type=F32).astype(BF16)
            rows[j, a, pl.ds(0, cap)] = got[:cap]
            for o in range(1, inner):
                sbuf[j, a, o - 1] = got[o * cap : (o + 1) * cap]
                x_copy(a, j, o).start()

    def nt(a, b):
        return lax.dot_general(a, b, (((1,), (1,)), ((), ())), preferred_element_type=F32)

    def work(k):
        j = source(k)
        for a in range(3):
            for o in range(1, inner):
                x_arrival(a, j, o).wait_recv()
        count = inner * cap
        both = rows[j, pl.ds(0, 2)].reshape(2 * count, rows.shape[3])
        up = jnp.dot(both, wu[...], preferred_element_type=F32)
        act = up[:count]
        act_tan = up[count:] + jnp.dot(rows[j, 0], vu[...], preferred_element_type=F32)
        s = 1.0 / (1.0 + jnp.exp(-act))
        s1 = s * (1.0 + act * (1.0 - s))
        s2 = s * (1.0 - s) * (2.0 + act * (1.0 - 2.0 * s))
        back = nt(rows[j, 2], wd[...])
        gz = (back * s1).astype(BF16)
        gzd = (back * s2 * act_tan).astype(BF16)
        hid[0, j] = (s1 * act_tan).astype(BF16)
        hid[1, j] = gz
        hid[2, j] = gzd
        ha = (nt(gzd, wu[...]) + nt(gz, vu[...])).astype(BF16)
        hback[j, pl.ds(0, cap)] = ha[:cap]
        for o in range(1, inner):
            hsend[j, o - 1] = ha[o * cap : (o + 1) * cap]
            h_copy(j, o).start()

    def give(k):
        j = source(k)
        for o in range(1, inner):
            h_arrival(j, o).wait_recv()
        ones, _ = picks(j)
        part = jnp.dot(ones.T.astype(BF16), hback[j], preferred_element_type=F32).astype(BF16)

        @pl.when(j == z)
        def _():
            pbuf[z] = part

        @pl.when(j != z)
        def _():
            psend[j] = part
            p_copy(j).start()

    def step(k, carry):
        @pl.when(k < n)
        def _():
            bring(k)

        @pl.when(k == 1)
        def _():
            for c in own[4:]:
                c.wait()

        @pl.when(jnp.logical_and(k >= 1, k < n + 1))
        def _():
            work(k - 1)

        @pl.when(k >= 2)
        def _():
            give(k - 2)

        return carry

    lax.fori_loop(0, n + 2, step, 0)

    for j in range(n):

        @pl.when(j != z)
        def _():
            p_arrival(j).wait_recv()

    total = pbuf[0].astype(F32)
    for j in range(1, n):
        total = total + pbuf[j].astype(F32)
    out[...] = total.astype(BF16)

    for a in range(4):

        @pl.when(has_left)
        def _():
            hop(a, z, z, own_send.at[a, 0]).wait_send()

        @pl.when(has_right)
        def _():
            hop(a, z, z, own_send.at[a, 1]).wait_send()

    for j in range(n):
        forwarded = jnp.logical_or(
            jnp.logical_and(j > z, has_left), jnp.logical_and(j < z, has_right)
        )

        @pl.when(forwarded)
        def _():
            for a in range(4):
                hop(a, j, z, fwd_send.at[a, j]).wait_send()

        for o in range(1, inner):
            for a in range(3):
                x_copy(a, j, o).wait_send()
            h_copy(j, o).wait_send()

        @pl.when(j != z)
        def _():
            p_copy(j).wait_send()


def per_device(tokens, tangents, cotangents, routes, gates, w_up, w_down, v_up):
    token_count, width = tokens.shape
    route_count = routes.shape[1]
    experts = lax.axis_size("expert")
    replicas = lax.axis_size("dp")
    hidden = w_up.shape[2]
    cap = max(2, token_count * route_count * 2 // experts)
    scale = 1.0 / math.sqrt(token_count * route_count * replicas)
    n = 4
    inner = experts // n
    meta = route_rows(routes, gates, experts)
    count = inner * cap
    vmem = pl.BlockSpec(memory_space=pltpu.VMEM)
    hbm = pl.BlockSpec(memory_space=pl.ANY)
    dma = pltpu.SemaphoreType.DMA
    hvp_tokens, rows, hid = pl.pallas_call(
        functools.partial(layer_kernel, n, inner, cap),
        out_shape=(
            jax.ShapeDtypeStruct((token_count, width), BF16),
            jax.ShapeDtypeStruct((n, 3, count, width), BF16),
            jax.ShapeDtypeStruct((3, n, count, hidden), BF16),
        ),
        in_specs=[hbm] * 7,
        out_specs=(vmem, vmem, vmem),
        scratch_shapes=[
            pltpu.VMEM((n, 2 * experts, token_count), F32),
            pltpu.VMEM((3, n, token_count, width), BF16),
            pltpu.VMEM((n, 3, inner - 1, cap, width), BF16),
            pltpu.VMEM((n, count, width), BF16),
            pltpu.VMEM((n, inner - 1, cap, width), BF16),
            pltpu.VMEM((n, token_count, width), BF16),
            pltpu.VMEM((n, token_count, width), BF16),
            pltpu.VMEM((width, hidden), BF16),
            pltpu.VMEM((hidden, width), BF16),
            pltpu.VMEM((width, hidden), BF16),
            dma((7,)),
            dma((4, 2)),
            dma((4, n)),
            dma((4, n)),
            dma((3, n, inner - 1)),
            dma((3, n, inner - 1)),
            dma((n, inner - 1)),
            dma((n, inner - 1)),
            dma((n,)),
            dma((n,)),
        ],
        compiler_params=pltpu.CompilerParams(
            collective_id=0, has_side_effects=True, vmem_limit_bytes=58 * 1024 * 1024
        ),
        cost_estimate=pl.CostEstimate(
            flops=12 * n * count * width * hidden, bytes_accessed=20_000_000, transcendentals=0
        ),
    )(meta, tokens, tangents, cotangents, w_up[0], w_down[0], v_up[0])

    def tn(a, b):
        return lax.dot_general(a, b, (((0,), (0,)), ((), ())), preferred_element_type=F32)

    primal, tangent, cotan = (rows[:, a].reshape(n * count, width) for a in range(3))
    hd, gz, gzd = (hid[a].reshape(n * count, hidden) for a in range(3))
    first = tn(tangent, gz) + tn(primal, gzd)
    second = tn(cotan, hd)
    summed = lax.psum_scatter(
        (jnp.concatenate([first, second], axis=1) * scale).astype(BF16),
        "dp",
        scatter_dimension=0,
        tiled=True,
    ).astype(F32)
    hvp_up = summed[:, :hidden].astype(BF16)[None]
    hvp_down = summed[:, hidden:].T.astype(BF16)[None]
    return (hvp_tokens, hvp_up, hvp_down)


def solution(mesh):
    in_specs = (P(("dp", "expert"), None),) * 5 + (P("expert", None, None),) * 3
    out_specs = (P(("dp", "expert"), None), P("expert", "dp", None), P("expert", None, "dp"))
    return jax.shard_map(
        per_device, mesh=mesh, in_specs=in_specs, out_specs=out_specs, check_vma=False
    )
```

time: 319 us -> 270 us (0.85)
  Pallas kernels: 0 us -> 164 us
  blocking collectives: 105 us -> 0 us
  local copies, waits for them, and re-layouts: 42.7 us -> 10.2 us
  matrix products: 36.8 us -> 10.8 us
  waiting for transfers between devices: 81.5 us -> 58.5 us
  starting transfers between devices: 16.4 us -> 0.04 us
  other arithmetic: 20.7 us -> 11.9 us
    pallas_call x0 -> x1, Pallas kernels: none -> 164 us  [per_device(): pl.pallas_call(functools.partial(layer_kernel, n, inner, cap), out_shape=...]
    all_to_all x2 -> x0, blocking collectives: 105 us -> none  [the longest x1 54 us: per_device(): lax.all_to_all(send_cotan, 'expert', split_axis=0, concat_axis=0, tiled=T...]
    all_to_all x3 -> x0, waiting for transfers between devices: 81.5 us -> none  [the longest x1 47.3 us: per_device(): lax.all_to_all(input_hvp.reshape(expert_count, capacity, width), 'expert'...]
    reduce_scatter x1, waiting for transfers between devices: 0.01 us -> 58.5 us  [per_device(): lax.psum_scatter((jnp.concatenate([first, second], axis=1) * scale).astyp...]
    gather x6 -> x0, local copies, waits for them, and re-layouts: 30.2 us -> none  [the longest x3 19.1 us: gather_slots(): picked = jnp.take(rows, safe, axis=0)]
    dot_general x9 -> x3, matrix products: 36.8 us -> 10.8 us  [tn(): lax.dot_general(a, b, (((0,), (0,)), ((), ())), preferred_element_type=F32)]
    all_to_all x3 -> x0, starting transfers between devices: 16.2 us -> none  [the longest x1 7.25 us: per_device(): lax.all_to_all(send_gate, 'expert', split_axis=0, concat_axis=0, tiled=True)]
    slice x1 -> x2, local copies, waits for them, and re-layouts: 0.21 us -> 5.74 us  [the longest x1 3.98 us: per_device(): rows[:, a].reshape(n * count, width)]
  transfers between devices with their start and end apart: 4 -> 1, of which waited for: 2 -> 1; matrix products, arithmetic and copies ran while one was open for 17% -> 0% of each run, Pallas kernels for 0% -> 0%
where the time goes in v1:
time: 270 us; the launch traced here: 269 us
  Pallas kernels  164 us (61%)
  waiting for transfers between devices  58.5 us (22%)
  between operations  14.1 us (5%)
  other arithmetic  11.9 us (4%)
  matrix products  10.8 us (4%)
  local copies, waits for them, and re-layouts  10.2 us (4%)
    pallas_call x1, Pallas kernels, per_device(): pl.pallas_call(functools.partial(layer_kernel, n, inner, cap), out_shape=...  164 us
    reduce_scatter x1, waiting for transfers between devices, per_device(): lax.psum_scatter((jnp.concatenate([first, second], axis=1) * scale).astyp...  58.5 us
    dot_general x3, matrix products, tn(): lax.dot_general(a, b, (((0,), (0,)), ((), ())), preferred_element_type=F32)  10.8 us
    convert_element_type x1, other arithmetic, per_device(): (jnp.concatenate([first, second], axis=1) * scale).astype(BF16)  9.07 us
  transfers between devices with their start and end apart: 1, of which 1 were waited for; matrix products, arithmetic and copies ran while one was open for 0% of the time, Pallas kernels for 0%

profile of v1, /device:TPU:0, one launch (start us, length us, event | category | flops | bytes accessed | tf_op | source)
XLA Modules:
  0.0 269.4 jit_solution(4011789013271952764)
XLA Ops:
  7.2 0.0 reduce-scatter.2.cloned.1.call-start
  7.2 0.7 fusion.1
  7.9 0.7 convert_element_type.25
  8.6 0.7 select_reduce_fusion
  9.2 0.1 copy.16
  9.3 0.2 reduce_window_sum.11
  9.6 0.6 pad_maximum_fusion.meta
  10.2 163.9 %shard_map.103 = (bf16[128,2048]{1,0:T(8,128)(2,1)}, bf16[4,3,128,2048]{3,2,1,0:T(8,128)(2,1)}, bf16[3,4,128,768]{3,2,1,0:T(8,128)(2,1)}) custom-call(f32[16,128]{1,0:T(8,128)} %pad_maximum_fusion.meta, bf16[128,2048]{1,0:T(8,128)(2,1)} %tok.1, bf16[128,2048]{1,0:T(8,128)(2,1)} %tan.1, bf16[128,2048]{1,0:T(8,128)(2,1)} %cot.1, bf16[2048,768]{1,0:T(8,128)(2,1)} %bitcast.31, ...), custom_call_target="tpu_custom_call" | custom-call | flops 9663676416 | bytes 20000000 | tf_op jit(solution)/shard_map/pallas_call | solution.py:336
  174.1 1.8 fusion.3
  175.8 4.0 %fusion.2 = (bf16[4,1,128,2048]{3,2,1,0:T(8,128)(2,1)S(1)}, bf16[4,1,128,2048]{3,2,1,0:T(8,128)(2,1)S(1)}, bf16[4,1,128,2048]{3,2,1,0:T(8,128)(2,1)S(1)}) fusion(bf16[4,3,128,2048]{3,2,1,0:T(8,128)(2,1)} %get-tuple-element.7), kind=kLoop, calls=%fused_computation.10 | loop fusion | bytes 12582912 | tf_op jit(solution)/shard_map/slice | solution.py:378
  179.8 4.5 %fusion.5 = f32[2048,768]{0,1:T(8,128)} fusion(bf16[512,2048]{1,0:T(8,128)(2,1)S(1)} %bitcast.26, bf16[512,768]{1,0:T(8,128)(2,1)S(1)} %bitcast.29), kind=kOutput, calls=%fused_computation.13 | convolution fusion | flops 1610612736 | bytes 9175040 | tf_op jit(solution)/shard_map/dot_general | solution.py:376
  184.3 1.8 fusion.4
  186.2 4.5 %convolution_add_fusion = f32[2048,768]{0,1:T(8,128)} fusion(f32[2048,768]{0,1:T(8,128)S(1)} %fusion.4, bf16[512,2048]{1,0:T(8,128)(2,1)S(1)} %bitcast.24, bf16[512,768]{1,0:T(8,128)(2,1)S(1)} %bitcast.27), kind=kOutput, calls=%fused_computation.2 | convolution fusion | flops 1612185600 | bytes 15466496 | tf_op jit(solution)/shard_map/dot_general | solution.py:376
  190.6 9.1 %fusion = bf16[2048,1536]{0,1:T(8,128)(2,1)} fusion(f32[2048,768]{0,1:T(8,128)} %fusion.5, f32[2048,768]{0,1:T(8,128)} %convolution_add_fusion), kind=kLoop, calls=%fused_computation.1 | loop fusion | flops 9437184 | bytes 18874368 | tf_op jit(solution)/shard_map/convert_element_type | solution.py:383
  199.7 0.0 reduce-scatter.2.cloned.1.call-update
  199.7 0.0 copy-start
  199.7 58.5 %reduce-scatter.2.cloned.1.call-done = bf16[512,1536]{0,1:T(8,128)(2,1)} async-done(((bf16[2048,1536]{0,1:T(8,128)(2,1)}), bf16[512,1536]{0,1:T(8,128)(2,1)}) %reduce-scatter.2.cloned.1.call-update) | async-done | bytes 1572880 | tf_op jit(solution)/shard_map/reduce_scatter | solution.py:382
  258.2 2.4 slice_bitcast_fusion
  260.6 1.2 copy.18
  261.7 0.0 copy-done
  261.7 0.8 copy.20
  (3 shorter events, 0.1 us)
Async XLA Ops:
  7.2 251.1 %reduce-scatter.2.cloned.1.call-start = ((), (), s32[]{:S(2)}) async-start(), calls=%async_computation.1 | async-start | bytes 7864320 | tf_op jit(solution)/shard_map/reduce_scatter | solution.py:382
  199.7 62.0 %copy-start = (bf16[128,2048]{1,0:T(8,128)(2,1)S(1)}, bf16[128,2048]{1,0:T(8,128)(2,1)}, u32[]{:S(2)}) copy-start(bf16[128,2048]{1,0:T(8,128)(2,1)} %get-tuple-element.26) | copy-start | bytes 1572868
Sparse Core Ops, SparseCore 0:
  199.8 58.3 reduce-scatter.1

commit v2 on v1

--- a/solution.py
+++ b/solution.py
@@ -24,23 +24,33 @@
 
 
 def layer_kernel(
-    n, inner, cap,
+    n, inner, cap, planes, scale,
     meta, tok, tan, cot, w_up, w_down, v_up,
-    out, rows, hid,
-    mbuf, gbuf, sbuf, hback, hsend, pbuf, psend, wu, wd, vu,
+    out, out_up, out_down,
+    rows, hid, mbuf, gbuf, sbuf, hback, pbuf, wu, wd, vu,
+    acc_up, acc_down, core_out_up, core_out_down, core_in_up, core_in_down,
+    plane_out_up, plane_out_down, plane_in_up, plane_in_down,
     load_sem, own_send, fwd_send, g_recv, x_send, x_recv, h_send, h_recv, p_send, p_recv,
+    core_send, core_recv, plane_send, plane_recv,
 ):
     me = lax.axis_index("expert")
     z = me // inner
     x = me % inner
     experts = n * inner
     tokens = gbuf.shape[2]
+    rep = lax.axis_index("dp")
+    y = rep // 2
+    core = rep % 2
+    part = acc_up.shape[1]
 
     def at(outer_pos, inner_pos):
         return {"expert": outer_pos * inner + inner_pos}
 
     def peer(o):
         return lax.rem(x + o, inner)
+
+    def plane(o):
+        return lax.rem(y + o, planes)
 
     own = [
         pltpu.make_async_copy(src, dst, load_sem.at[i])
@@ -77,7 +87,15 @@
         def _():
             pl.semaphore_signal(barrier, inc=1, device_id=at(far, x), device_id_type=MESH)
 
-    pl.semaphore_wait(barrier, n - 1 + inner - 1)
+    pl.semaphore_signal(
+        barrier, inc=1, device_id={"dp": y * 2 + 1 - core}, device_id_type=MESH
+    )
+    for o in range(1, planes):
+        pl.semaphore_signal(
+            barrier, inc=1, device_id={"dp": plane(o) * 2 + core}, device_id_type=MESH
+        )
+
+    pl.semaphore_wait(barrier, n - 1 + inner - 1 + planes)
 
     def block(a, j):
         return mbuf.at[j] if a == 0 else gbuf.at[a - 1, j]
@@ -102,6 +120,9 @@
         @pl.when(has_right)
         def _():
             hop(a, z, z + 1, own_send.at[a, 1]).start()
+
+    acc_up[...] = jnp.zeros_like(acc_up)
+    acc_down[...] = jnp.zeros_like(acc_down)
 
     near = jnp.minimum(z, n - 1 - z)
     left_half = z < n - 1 - z
@@ -144,7 +165,7 @@
 
     def h_copy(j, o):
         return pltpu.make_async_remote_copy(
-            src_ref=hsend.at[j, o - 1],
+            src_ref=sbuf.at[j, 0, o - 1],
             dst_ref=hback.at[j, pl.ds((inner - o) * cap, cap)],
             send_sem=h_send.at[j, o - 1],
             recv_sem=h_recv.at[j, inner - o - 1],
@@ -154,7 +175,7 @@
 
     def h_arrival(j, o):
         return pltpu.make_async_remote_copy(
-            src_ref=hsend.at[j, o - 1],
+            src_ref=sbuf.at[j, 0, o - 1],
             dst_ref=hback.at[j, pl.ds(o * cap, cap)],
             send_sem=h_send.at[j, o - 1],
             recv_sem=h_recv.at[j, o - 1],
@@ -164,21 +185,21 @@
 
     def p_copy(j):
         return pltpu.make_async_remote_copy(
-            src_ref=psend.at[j],
-            dst_ref=pbuf.at[z],
+            src_ref=gbuf.at[0, j],
+            dst_ref=pbuf.at[lax.rem(z - j + n, n) - 1],
             send_sem=p_send.at[j],
-            recv_sem=p_recv.at[z],
+            recv_sem=p_recv.at[lax.rem(z - j + n, n) - 1],
             device_id=at(j, x),
             device_id_type=MESH,
         )
 
-    def p_arrival(j):
-        return pltpu.make_async_remote_copy(
-            src_ref=psend.at[j],
-            dst_ref=pbuf.at[j],
-            send_sem=p_send.at[j],
-            recv_sem=p_recv.at[j],
-            device_id=at(j, x),
+    def p_arrival(o):
+        return pltpu.make_async_remote_copy(
+            src_ref=gbuf.at[0, lax.rem(z + o, n)],
+            dst_ref=pbuf.at[o - 1],
+            send_sem=p_send.at[lax.rem(z + o, n)],
+            recv_sem=p_recv.at[o - 1],
+            device_id=at(lax.rem(z + o, n), x),
             device_id_type=MESH,
         )
 
@@ -213,6 +234,76 @@
 
     def nt(a, b):
         return lax.dot_general(a, b, (((1,), (1,)), ((), ())), preferred_element_type=F32)
+
+    def tn(a, b):
+        return lax.dot_general(a, b, (((0,), (0,)), ((), ())), preferred_element_type=F32)
+
+    def part_up(j, c):
+        columns = pl.ds(pl.multiple_of(c * part, part), part)
+        left = rows[j, pl.ds(0, 2), :, columns].reshape(2 * inner * cap, part)
+        return tn(left, hid[j, pl.ds(0, 2)].reshape(2 * inner * cap, hid.shape[3]))
+
+    def part_down(j, c):
+        columns = pl.ds(pl.multiple_of(c * part, part), part)
+        return tn(hid[j, 2], rows[j, 2, :, columns])
+
+    def gather_part(j, c, carry):
+        acc_up[c] += part_up(j, c)
+        acc_down[c] += part_down(j, c)
+        return carry
+
+    core_out, core_in = (core_out_up, core_out_down), (core_in_up, core_in_down)
+    plane_out, plane_in = (plane_out_up, plane_out_down), (plane_in_up, plane_in_down)
+    accs, parts = (acc_up, acc_down), (part_up, part_down)
+
+    def core_copy(half, yy):
+        return pltpu.make_async_remote_copy(
+            src_ref=core_out[half].at[yy],
+            dst_ref=core_in[half].at[yy],
+            send_sem=core_send.at[half, yy],
+            recv_sem=core_recv.at[half, yy],
+            device_id={"dp": y * 2 + 1 - core},
+            device_id_type=MESH,
+        )
+
+    def plane_copy(half, o):
+        return pltpu.make_async_remote_copy(
+            src_ref=plane_out[half].at[o - 1],
+            dst_ref=plane_in[half].at[planes - o - 1],
+            send_sem=plane_send.at[half, o - 1],
+            recv_sem=plane_recv.at[half, planes - o - 1],
+            device_id={"dp": plane(o) * 2 + core},
+            device_id_type=MESH,
+        )
+
+    def plane_arrival(half, o):
+        return pltpu.make_async_remote_copy(
+            src_ref=plane_out[half].at[o - 1],
+            dst_ref=plane_in[half].at[o - 1],
+            send_sem=plane_send.at[half, o - 1],
+            recv_sem=plane_recv.at[half, o - 1],
+            device_id={"dp": plane(o) * 2 + core},
+            device_id_type=MESH,
+        )
+
+    def share(j):
+        for o in range(1, planes + 1):
+            yy = plane(o)
+            for half in range(2):
+                c = yy * 2 + 1 - core
+                mine = accs[half][c] + parts[half](j, c)
+                core_out[half][yy] = (mine * scale).astype(BF16)
+                core_copy(half, yy).start()
+            for half in range(2):
+                c = yy * 2 + core
+                mine = (accs[half][c] + parts[half](j, c)) * scale
+                if o < planes:
+                    core_copy(half, yy).wait_recv()
+                    mine = mine + core_in[half][yy].astype(F32)
+                    plane_out[half][o - 1] = mine.astype(BF16)
+                    plane_copy(half, o).start()
+                else:
+                    accs[half][c] = mine
 
     def work(k):
         j = source(k)
@@ -230,14 +321,41 @@
         back = nt(rows[j, 2], wd[...])
         gz = (back * s1).astype(BF16)
         gzd = (back * s2 * act_tan).astype(BF16)
-        hid[0, j] = (s1 * act_tan).astype(BF16)
-        hid[1, j] = gz
-        hid[2, j] = gzd
+        hid[j, 0] = gzd
+        hid[j, 1] = gz
+        hid[j, 2] = (s1 * act_tan).astype(BF16)
+
+        @pl.when(k == n - 1)
+        def _():
+            share(j)
+
         ha = (nt(gzd, wu[...]) + nt(gz, vu[...])).astype(BF16)
         hback[j, pl.ds(0, cap)] = ha[:cap]
         for o in range(1, inner):
-            hsend[j, o - 1] = ha[o * cap : (o + 1) * cap]
+            x_copy(0, j, o).wait_send()
+            sbuf[j, 0, o - 1] = ha[o * cap : (o + 1) * cap]
             h_copy(j, o).start()
+
+        @pl.when(k < n - 1)
+        def _():
+            lax.fori_loop(0, 2 * planes, functools.partial(gather_part, j), 0)
+
+    def sent(a, j):
+        @pl.when(jnp.logical_and(j == z, has_left))
+        def _():
+            hop(a, z, z, own_send.at[a, 0]).wait_send()
+
+        @pl.when(jnp.logical_and(j == z, has_right))
+        def _():
+            hop(a, z, z, own_send.at[a, 1]).wait_send()
+
+        forwarded = jnp.logical_or(
+            jnp.logical_and(j > z, has_left), jnp.logical_and(j < z, has_right)
+        )
+
+        @pl.when(forwarded)
+        def _():
+            hop(a, j, z, fwd_send.at[a, j]).wait_send()
 
     def give(k):
         j = source(k)
@@ -246,13 +364,11 @@
         ones, _ = picks(j)
         part = jnp.dot(ones.T.astype(BF16), hback[j], preferred_element_type=F32).astype(BF16)
 
-        @pl.when(j == z)
-        def _():
-            pbuf[z] = part
+        sent(1, j)
+        gbuf[0, j] = part
 
         @pl.when(j != z)
         def _():
-            psend[j] = part
             p_copy(j).start()
 
     def step(k, carry):
@@ -277,39 +393,30 @@
 
     lax.fori_loop(0, n + 2, step, 0)
 
+    total = gbuf[0, z].astype(F32)
+    for o in range(1, n):
+        p_arrival(o).wait_recv()
+        total = total + pbuf[o - 1].astype(F32)
+    out[...] = total.astype(BF16)
+
+    for half, result in enumerate((out_up, out_down)):
+        core_copy(half, y).wait_recv()
+        total = accs[half][y * 2 + core] + core_in[half][y].astype(F32)
+        for o in range(1, planes):
+            plane_arrival(half, o).wait_recv()
+            total = total + plane_in[half][o - 1].astype(F32)
+        result[...] = total.astype(BF16)
+        for o in range(1, planes):
+            plane_copy(half, o).wait_send()
+        for yy in range(planes):
+            core_copy(half, yy).wait_send()
+
     for j in range(n):
-
-        @pl.when(j != z)
-        def _():
-            p_arrival(j).wait_recv()
-
-    total = pbuf[0].astype(F32)
-    for j in range(1, n):
-        total = total + pbuf[j].astype(F32)
-    out[...] = total.astype(BF16)
-
-    for a in range(4):
-
-        @pl.when(has_left)
-        def _():
-            hop(a, z, z, own_send.at[a, 0]).wait_send()
-
-        @pl.when(has_right)
-        def _():
-            hop(a, z, z, own_send.at[a, 1]).wait_send()
-
-    for j in range(n):
-        forwarded = jnp.logical_or(
-            jnp.logical_and(j > z, has_left), jnp.logical_and(j < z, has_right)
-        )
-
-        @pl.when(forwarded)
-        def _():
-            for a in range(4):
-                hop(a, j, z, fwd_send.at[a, j]).wait_send()
+        for a in (0, 2, 3):
+            sent(a, j)
 
         for o in range(1, inner):
-            for a in range(3):
+            for a in range(1, 3):
                 x_copy(a, j, o).wait_send()
             h_copy(j, o).wait_send()
 
@@ -330,29 +437,42 @@
     inner = experts // n
     meta = route_rows(routes, gates, experts)
     count = inner * cap
+    planes = replicas // 2
+    part = width // replicas
     vmem = pl.BlockSpec(memory_space=pltpu.VMEM)
     hbm = pl.BlockSpec(memory_space=pl.ANY)
     dma = pltpu.SemaphoreType.DMA
-    hvp_tokens, rows, hid = pl.pallas_call(
-        functools.partial(layer_kernel, n, inner, cap),
+    up, down = (part, hidden), (hidden, part)
+    hvp_tokens, hvp_up, hvp_down = pl.pallas_call(
+        functools.partial(layer_kernel, n, inner, cap, planes, scale),
         out_shape=(
             jax.ShapeDtypeStruct((token_count, width), BF16),
-            jax.ShapeDtypeStruct((n, 3, count, width), BF16),
-            jax.ShapeDtypeStruct((3, n, count, hidden), BF16),
+            jax.ShapeDtypeStruct(up, BF16),
+            jax.ShapeDtypeStruct(down, BF16),
         ),
         in_specs=[hbm] * 7,
         out_specs=(vmem, vmem, vmem),
         scratch_shapes=[
+            pltpu.VMEM((n, 3, count, width), BF16),
+            pltpu.VMEM((n, 3, count, hidden), BF16),
             pltpu.VMEM((n, 2 * experts, token_count), F32),
             pltpu.VMEM((3, n, token_count, width), BF16),
             pltpu.VMEM((n, 3, inner - 1, cap, width), BF16),
             pltpu.VMEM((n, count, width), BF16),
-            pltpu.VMEM((n, inner - 1, cap, width), BF16),
-            pltpu.VMEM((n, token_count, width), BF16),
-            pltpu.VMEM((n, token_count, width), BF16),
+            pltpu.VMEM((n - 1, token_count, width), BF16),
             pltpu.VMEM((width, hidden), BF16),
             pltpu.VMEM((hidden, width), BF16),
             pltpu.VMEM((width, hidden), BF16),
+            pltpu.VMEM((replicas,) + up, F32),
+            pltpu.VMEM((replicas,) + down, F32),
+            pltpu.VMEM((planes,) + up, BF16),
+            pltpu.VMEM((planes,) + down, BF16),
+            pltpu.VMEM((planes,) + up, BF16),
+            pltpu.VMEM((planes,) + down, BF16),
+            pltpu.VMEM((planes - 1,) + up, BF16),
+            pltpu.VMEM((planes - 1,) + down, BF16),
+            pltpu.VMEM((planes - 1,) + up, BF16),
+            pltpu.VMEM((planes - 1,) + down, BF16),
             dma((7,)),
             dma((4, 2)),
             dma((4, n)),
@@ -363,31 +483,19 @@
             dma((n, inner - 1)),
             dma((n,)),
             dma((n,)),
+            dma((2, planes)),
+            dma((2, planes)),
+            dma((2, planes - 1)),
+            dma((2, planes - 1)),
         ],
         compiler_params=pltpu.CompilerParams(
-            collective_id=0, has_side_effects=True, vmem_limit_bytes=58 * 1024 * 1024
+            collective_id=0, has_side_effects=True, vmem_limit_bytes=61 * 1024 * 1024
         ),
         cost_estimate=pl.CostEstimate(
-            flops=12 * n * count * width * hidden, bytes_accessed=20_000_000, transcendentals=0
+            flops=18 * n * count * width * hidden, bytes_accessed=20_000_000, transcendentals=0
         ),
     )(meta, tokens, tangents, cotangents, w_up[0], w_down[0], v_up[0])
-
-    def tn(a, b):
-        return lax.dot_general(a, b, (((0,), (0,)), ((), ())), preferred_element_type=F32)
-
-    primal, tangent, cotan = (rows[:, a].reshape(n * count, width) for a in range(3))
-    hd, gz, gzd = (hid[a].reshape(n * count, hidden) for a in range(3))
-    first = tn(tangent, gz) + tn(primal, gzd)
-    second = tn(cotan, hd)
-    summed = lax.psum_scatter(
-        (jnp.concatenate([first, second], axis=1) * scale).astype(BF16),
-        "dp",
-        scatter_dimension=0,
-        tiled=True,
-    ).astype(F32)
-    hvp_up = summed[:, :hidden].astype(BF16)[None]
-    hvp_down = summed[:, hidden:].T.astype(BF16)[None]
-    return (hvp_tokens, hvp_up, hvp_down)
+    return (hvp_tokens, hvp_up[None], hvp_down[None])
 
 
 def solution(mesh):

time: 270 us -> 168 us (0.62)
  waiting for transfers between devices: 58.5 us -> 0 us
  between operations: 14.1 us -> 0.65 us
  matrix products: 10.8 us -> 0 us
  other arithmetic: 11.9 us -> 2.84 us
  local copies, waits for them, and re-layouts: 10.2 us -> 5.05 us
  Pallas kernels: 164 us -> 159 us
    reduce_scatter x1 -> x0, waiting for transfers between devices: 58.5 us -> none  [per_device(): lax.psum_scatter((jnp.concatenate([first, second], axis=1) * scale).astyp...]
    dot_general x3 -> x0, matrix products: 10.8 us -> none  [tn(): lax.dot_general(a, b, (((0,), (0,)), ((), ())), preferred_element_type=F32)]
    convert_element_type x1 -> x0, other arithmetic: 9.07 us -> none  [per_device(): (jnp.concatenate([first, second], axis=1) * scale).astype(BF16)]
    slice x2 -> x0, local copies, waits for them, and re-layouts: 5.74 us -> none  [the longest x1 3.98 us: per_device(): rows[:, a].reshape(n * count, width)]
    pallas_call x1, Pallas kernels: 164 us -> 159 us  [per_device(): pl.pallas_call(functools.partial(layer_kernel, n, inner, cap, planes, sca...]
    unnamed x4 -> x5, local copies, waits for them, and re-layouts: 1.95 us -> 4.9 us
  transfers between devices with their start and end apart: 1 -> 0, of which waited for: 1 -> 0; matrix products, arithmetic and copies ran while one was open for 0% -> 0% of each run, Pallas kernels for 0% -> 0%
where the time goes in v2:
time: 168 us
  Pallas kernels  159 us (95%)
  local copies, waits for them, and re-layouts  5.05 us (3%)
  other arithmetic  2.84 us (2%)
    pallas_call x1, Pallas kernels, per_device(): pl.pallas_call(functools.partial(layer_kernel, n, inner, cap, planes, sca...  159 us
    unnamed x5, local copies, waits for them, and re-layouts  4.9 us

profile of v2, /device:TPU:0, one launch (start us, length us, event | category | flops | bytes accessed | tf_op | source)
XLA Modules:
  0.0 167.7 jit_solution(14440943300058034361)
XLA Ops:
  0.6 0.7 fusion
  1.3 0.7 convert_element_type.16
  2.0 0.7 select_reduce_fusion
  2.7 0.1 copy.15
  2.8 0.2 reduce_window_sum.11
  3.0 0.6 pad_maximum_fusion.meta
  3.6 159.1 %shard_map.103 = (bf16[128,2048]{1,0:T(8,128)(2,1)}, bf16[512,768]{1,0:T(8,128)(2,1)}, bf16[768,512]{1,0:T(8,128)(2,1)}) custom-call(f32[16,128]{1,0:T(8,128)} %pad_maximum_fusion.meta, bf16[128,2048]{1,0:T(8,128)(2,1)} %tok.1, bf16[128,2048]{1,0:T(8,128)(2,1)} %tan.1, bf16[128,2048]{1,0:T(8,128)(2,1)} %cot.1, bf16[2048,768]{1,0:T(8,128)(2,1)} %bitcast.11, ...), custom_call_target="tpu_custom_call" | custom-call | flops 14495514624 | bytes 20000000 | tf_op jit(solution)/shard_map/pallas_call | solution.py:446
  162.8 0.0 copy-start
  162.8 2.0 %copy.20 = bf16[128,2048]{1,0:T(8,128)(2,1)} copy(bf16[128,2048]{1,0:T(8,128)(2,1)} %get-tuple-element.12) | data formatting | bytes 1048576
  164.7 2.1 %copy.21 = bf16[1,512,768]{2,1,0:T(8,128)(2,1)} copy(bf16[1,512,768]{2,1,0:T(8,128)(2,1)} %bitcast.9) | data formatting | bytes 1572864
  166.8 0.0 copy-done
  166.8 0.9 copy.22
  (3 shorter events, 0.1 us)
Async XLA Ops:
  162.8 4.0 %copy-start = (bf16[768,512]{1,0:T(8,128)(2,1)S(1)}, bf16[768,512]{1,0:T(8,128)(2,1)}, u32[]{:S(2)}) copy-start(bf16[768,512]{1,0:T(8,128)(2,1)} %get-tuple-element.8) | copy-start | bytes 2359300

commit v3 on v2

--- a/solution.py
+++ b/solution.py
@@ -28,10 +28,9 @@
     meta, tok, tan, cot, w_up, w_down, v_up,
     out, out_up, out_down,
     rows, hid, mbuf, gbuf, sbuf, hback, pbuf, wu, wd, vu,
-    acc_up, acc_down, core_out_up, core_out_down, core_in_up, core_in_down,
-    plane_out_up, plane_out_down, plane_in_up, plane_in_down,
+    acc_up, acc_down, far_rows, far_hid,
     load_sem, own_send, fwd_send, g_recv, x_send, x_recv, h_send, h_recv, p_send, p_recv,
-    core_send, core_recv, plane_send, plane_recv,
+    row_send, row_recv, hid_send, hid_recv,
 ):
     me = lax.axis_index("expert")
     z = me // inner
@@ -41,7 +40,10 @@
     rep = lax.axis_index("dp")
     y = rep // 2
     core = rep % 2
-    part = acc_up.shape[1]
+    part = acc_up.shape[0]
+    replicas = 2 * planes
+    sibling = y * 2 + 1 - core
+    count = inner * cap
 
     def at(outer_pos, inner_pos):
         return {"expert": outer_pos * inner + inner_pos}
@@ -87,15 +89,12 @@
         def _():
             pl.semaphore_signal(barrier, inc=1, device_id=at(far, x), device_id_type=MESH)
 
-    pl.semaphore_signal(
-        barrier, inc=1, device_id={"dp": y * 2 + 1 - core}, device_id_type=MESH
-    )
-    for o in range(1, planes):
+    for f in range(1, replicas):
         pl.semaphore_signal(
-            barrier, inc=1, device_id={"dp": plane(o) * 2 + core}, device_id_type=MESH
-        )
-
-    pl.semaphore_wait(barrier, n - 1 + inner - 1 + planes)
+            barrier, inc=1, device_id={"dp": lax.rem(rep + f, replicas)}, device_id_type=MESH
+        )
+
+    pl.semaphore_wait(barrier, n - 1 + inner - 1 + replicas - 1)
 
     def block(a, j):
         return mbuf.at[j] if a == 0 else gbuf.at[a - 1, j]
@@ -203,34 +202,28 @@
             device_id_type=MESH,
         )
 
-    def bring(k):
-        j = source(k)
+    def take(a, j):
         forward_left = jnp.logical_and(j > z, has_left)
         forward_right = jnp.logical_and(j < z, has_right)
 
-        def take(a):
-            @pl.when(j != z)
+        @pl.when(j != z)
+        def _():
+            hop(a, j, z, fwd_send.at[a, j]).wait_recv()
+
+            @pl.when(forward_left)
             def _():
-                hop(a, j, z, fwd_send.at[a, j]).wait_recv()
-
-                @pl.when(forward_left)
-                def _():
-                    hop(a, j, z - 1, fwd_send.at[a, j]).start()
-
-                @pl.when(forward_right)
-                def _():
-                    hop(a, j, z + 1, fwd_send.at[a, j]).start()
-
-        take(0)
-        ones, gated = picks(j)
-        for a in range(3):
-            take(a + 1)
-            pick = (gated if a == 2 else ones).astype(BF16)
-            got = jnp.dot(pick, gbuf[a, j], preferred_element_type=F32).astype(BF16)
-            rows[j, a, pl.ds(0, cap)] = got[:cap]
-            for o in range(1, inner):
-                sbuf[j, a, o - 1] = got[o * cap : (o + 1) * cap]
-                x_copy(a, j, o).start()
+                hop(a, j, z - 1, fwd_send.at[a, j]).start()
+
+            @pl.when(forward_right)
+            def _():
+                hop(a, j, z + 1, fwd_send.at[a, j]).start()
+
+    def pass_on(a, j, pick):
+        got = jnp.dot(pick.astype(BF16), gbuf[a, j], preferred_element_type=F32).astype(BF16)
+        for o in range(1, inner):
+            sbuf[j, a, o - 1] = got[o * cap : (o + 1) * cap]
+            x_copy(a, j, o).start()
+        rows[j, a, pl.ds(0, cap)] = got[:cap]
 
     def nt(a, b):
         return lax.dot_general(a, b, (((1,), (1,)), ((), ())), preferred_element_type=F32)
@@ -238,79 +231,125 @@
     def tn(a, b):
         return lax.dot_general(a, b, (((0,), (0,)), ((), ())), preferred_element_type=F32)
 
-    def part_up(j, c):
-        columns = pl.ds(pl.multiple_of(c * part, part), part)
-        left = rows[j, pl.ds(0, 2), :, columns].reshape(2 * inner * cap, part)
-        return tn(left, hid[j, pl.ds(0, 2)].reshape(2 * inner * cap, hid.shape[3]))
-
-    def part_down(j, c):
-        columns = pl.ds(pl.multiple_of(c * part, part), part)
-        return tn(hid[j, 2], rows[j, 2, :, columns])
-
-    def gather_part(j, c, carry):
-        acc_up[c] += part_up(j, c)
-        acc_down[c] += part_down(j, c)
-        return carry
-
-    core_out, core_in = (core_out_up, core_out_down), (core_in_up, core_in_down)
-    plane_out, plane_in = (plane_out_up, plane_out_down), (plane_in_up, plane_in_down)
-    accs, parts = (acc_up, acc_down), (part_up, part_down)
-
-    def core_copy(half, yy):
-        return pltpu.make_async_remote_copy(
-            src_ref=core_out[half].at[yy],
-            dst_ref=core_in[half].at[yy],
-            send_sem=core_send.at[half, yy],
-            recv_sem=core_recv.at[half, yy],
-            device_id={"dp": y * 2 + 1 - core},
-            device_id_type=MESH,
-        )
-
-    def plane_copy(half, o):
-        return pltpu.make_async_remote_copy(
-            src_ref=plane_out[half].at[o - 1],
-            dst_ref=plane_in[half].at[planes - o - 1],
-            send_sem=plane_send.at[half, o - 1],
-            recv_sem=plane_recv.at[half, planes - o - 1],
-            device_id={"dp": plane(o) * 2 + core},
-            device_id_type=MESH,
-        )
-
-    def plane_arrival(half, o):
-        return pltpu.make_async_remote_copy(
-            src_ref=plane_out[half].at[o - 1],
-            dst_ref=plane_in[half].at[o - 1],
-            send_sem=plane_send.at[half, o - 1],
-            recv_sem=plane_recv.at[half, o - 1],
-            device_id={"dp": plane(o) * 2 + core},
-            device_id_type=MESH,
-        )
-
-    def share(j):
-        for o in range(1, planes + 1):
-            yy = plane(o)
-            for half in range(2):
-                c = yy * 2 + 1 - core
-                mine = accs[half][c] + parts[half](j, c)
-                core_out[half][yy] = (mine * scale).astype(BF16)
-                core_copy(half, yy).start()
-            for half in range(2):
-                c = yy * 2 + core
-                mine = (accs[half][c] + parts[half](j, c)) * scale
-                if o < planes:
-                    core_copy(half, yy).wait_recv()
-                    mine = mine + core_in[half][yy].astype(F32)
-                    plane_out[half][o - 1] = mine.astype(BF16)
-                    plane_copy(half, o).start()
-                else:
-                    accs[half][c] = mine
-
-    def work(k):
+    def columns(r):
+        return pl.ds(pl.multiple_of(r * part, part), part)
+
+    def place(there, sender):
+        return lax.rem(sender - there + replicas, replicas) - 1
+
+    def row_copy(a, j, f):
+        r = lax.rem(rep + f, replicas)
+        return pltpu.make_async_remote_copy(
+            src_ref=rows.at[j, a, :, columns(r)],
+            dst_ref=far_rows.at[j, a, replicas - f - 1],
+            send_sem=row_send.at[a, j, f - 1],
+            recv_sem=row_recv.at[a, j, replicas - f - 1],
+            device_id={"dp": r},
+            device_id_type=MESH,
+        )
+
+    def row_arrival(a, j, f):
+        return pltpu.make_async_remote_copy(
+            src_ref=rows.at[j, a, :, columns(rep)],
+            dst_ref=far_rows.at[j, a, f - 1],
+            send_sem=row_send.at[a, j, f - 1],
+            recv_sem=row_recv.at[a, j, f - 1],
+            device_id={"dp": lax.rem(rep + f, replicas)},
+            device_id_type=MESH,
+        )
+
+    def hid_copy(h, j, o):
+        r = sibling if o == 0 else plane(o) * 2 + core
+        return pltpu.make_async_remote_copy(
+            src_ref=hid.at[j, h],
+            dst_ref=far_hid.at[j, h, place(r, rep)],
+            send_sem=hid_send.at[h, j, place(rep, r)],
+            recv_sem=hid_recv.at[h, j, place(r, rep)],
+            device_id={"dp": r},
+            device_id_type=MESH,
+        )
+
+    def hid_relay(h, j, o):
+        d = plane(o) * 2 + core
+        return pltpu.make_async_remote_copy(
+            src_ref=far_hid.at[j, h, place(rep, d)],
+            dst_ref=far_hid.at[j, h, place(sibling, d)],
+            send_sem=hid_send.at[h, j, place(rep, plane(o) * 2 + 1 - core)],
+            recv_sem=hid_recv.at[h, j, place(sibling, d)],
+            device_id={"dp": sibling},
+            device_id_type=MESH,
+        )
+
+    def hid_arrival(h, j, d):
+        return pltpu.make_async_remote_copy(
+            src_ref=hid.at[j, h],
+            dst_ref=far_hid.at[j, h, place(rep, d)],
+            send_sem=hid_send.at[h, j, place(rep, d)],
+            recv_sem=hid_recv.at[h, j, place(rep, d)],
+            device_id={"dp": d},
+            device_id_type=MESH,
+        )
+
+    def relay(h, j):
+        for o in range(1, planes):
+            hid_arrival(h, j, plane(o) * 2 + core).wait_recv()
+            hid_relay(h, j, o).start()
+
+    def absorb(j):
+        depth = (replicas - 1) * count
+        acc_down[...] += tn(hid[j, 2], rows[j, 2, :, columns(rep)])
+        acc_up[...] += tn(
+            rows[j, pl.ds(0, 2), :, columns(rep)].reshape(2 * count, part),
+            hid[j, pl.ds(0, 2)].reshape(2 * count, hid.shape[3]),
+        )
+
+        def arrived(i):
+            for f in range(1, replicas):
+                row_arrival(i, j, f).wait_recv()
+            for o in range(planes):
+                hid_arrival(i, j, sibling if o == 0 else plane(o) * 2 + 1 - core).wait_recv()
+
+        arrived(2)
+        acc_down[...] += tn(
+            far_hid[j, 2].reshape(depth, hid.shape[3]), far_rows[j, 2].reshape(depth, part)
+        )
+        arrived(1)
+        arrived(0)
+        acc_up[...] += tn(
+            far_rows[j, pl.ds(0, 2)].reshape(2 * depth, part),
+            far_hid[j, pl.ds(0, 2)].reshape(2 * depth, hid.shape[3]),
+        )
+
+    def landed(a, j):
+        for o in range(1, inner):
+            x_arrival(a, j, o).wait_recv()
+        for f in range(1, replicas):
+            row_copy(a, j, f).start()
+
+    def send_hidden(h, j, value):
+        hid[j, h] = value.astype(BF16)
+        for o in range(1, planes):
+            hid_copy(h, j, o).start()
+        hid_copy(h, j, 0).start()
+
+    def first_part(k):
         j = source(k)
-        for a in range(3):
-            for o in range(1, inner):
-                x_arrival(a, j, o).wait_recv()
-        count = inner * cap
+        take(0, j)
+        ones, _ = picks(j)
+        for a in range(2):
+            take(a + 1, j)
+            pass_on(a, j, ones)
+
+    def second_part(k):
+        j = source(k)
+
+        @pl.when(k == 0)
+        def _():
+            own[4].wait()
+            own[5].wait()
+
+        landed(0, j)
+        landed(1, j)
         both = rows[j, pl.ds(0, 2)].reshape(2 * count, rows.shape[3])
         up = jnp.dot(both, wu[...], preferred_element_type=F32)
         act = up[:count]
@@ -318,27 +357,27 @@
         s = 1.0 / (1.0 + jnp.exp(-act))
         s1 = s * (1.0 + act * (1.0 - s))
         s2 = s * (1.0 - s) * (2.0 + act * (1.0 - 2.0 * s))
+        s2_tan = s2 * act_tan
+        send_hidden(2, j, s1 * act_tan)
+
+        take(3, j)
+        _, gated = picks(j)
+        pass_on(2, j, gated)
+
+        @pl.when(k == 0)
+        def _():
+            own[6].wait()
+
+        landed(2, j)
         back = nt(rows[j, 2], wd[...])
-        gz = (back * s1).astype(BF16)
-        gzd = (back * s2 * act_tan).astype(BF16)
-        hid[j, 0] = gzd
-        hid[j, 1] = gz
-        hid[j, 2] = (s1 * act_tan).astype(BF16)
-
-        @pl.when(k == n - 1)
-        def _():
-            share(j)
-
-        ha = (nt(gzd, wu[...]) + nt(gz, vu[...])).astype(BF16)
-        hback[j, pl.ds(0, cap)] = ha[:cap]
+        send_hidden(1, j, back * s1)
+        send_hidden(0, j, back * s2_tan)
+        ha = (nt(hid[j, 0], wu[...]) + nt(hid[j, 1], vu[...])).astype(BF16)
         for o in range(1, inner):
             x_copy(0, j, o).wait_send()
             sbuf[j, 0, o - 1] = ha[o * cap : (o + 1) * cap]
             h_copy(j, o).start()
-
-        @pl.when(k < n - 1)
-        def _():
-            lax.fori_loop(0, 2 * planes, functools.partial(gather_part, j), 0)
+        hback[j, pl.ds(0, cap)] = ha[:cap]
 
     def sent(a, j):
         @pl.when(jnp.logical_and(j == z, has_left))
@@ -357,8 +396,7 @@
         def _():
             hop(a, j, z, fwd_send.at[a, j]).wait_send()
 
-    def give(k):
-        j = source(k)
+    def give(j):
         for o in range(1, inner):
             h_arrival(j, o).wait_recv()
         ones, _ = picks(j)
@@ -374,24 +412,27 @@
     def step(k, carry):
         @pl.when(k < n)
         def _():
-            bring(k)
-
-        @pl.when(k == 1)
-        def _():
-            for c in own[4:]:
-                c.wait()
-
-        @pl.when(jnp.logical_and(k >= 1, k < n + 1))
-        def _():
-            work(k - 1)
-
-        @pl.when(k >= 2)
-        def _():
-            give(k - 2)
+            first_part(k)
+
+        @pl.when(k >= 1)
+        def _():
+            j = source(k - 1)
+            relay(2, j)
+            give(j)
+            relay(1, j)
+            relay(0, j)
+            absorb(j)
+
+        @pl.when(k < n)
+        def _():
+            second_part(k)
 
         return carry
 
-    lax.fori_loop(0, n + 2, step, 0)
+    lax.fori_loop(0, n + 1, step, 0)
+
+    out_up[...] = (acc_up[...] * scale).astype(BF16)
+    out_down[...] = (acc_down[...] * scale).astype(BF16)
 
     total = gbuf[0, z].astype(F32)
     for o in range(1, n):
@@ -399,19 +440,7 @@
         total = total + pbuf[o - 1].astype(F32)
     out[...] = total.astype(BF16)
 
-    for half, result in enumerate((out_up, out_down)):
-        core_copy(half, y).wait_recv()
-        total = accs[half][y * 2 + core] + core_in[half][y].astype(F32)
-        for o in range(1, planes):
-            plane_arrival(half, o).wait_recv()
-            total = total + plane_in[half][o - 1].astype(F32)
-        result[...] = total.astype(BF16)
-        for o in range(1, planes):
-            plane_copy(half, o).wait_send()
-        for yy in range(planes):
-            core_copy(half, yy).wait_send()
-
-    for j in range(n):
+    def drain(j, carry):
         for a in (0, 2, 3):
             sent(a, j)
 
@@ -423,6 +452,18 @@
         @pl.when(j != z)
         def _():
             p_copy(j).wait_send()
+
+        for a in range(3):
+            for f in range(1, replicas):
+                row_copy(a, j, f).wait_send()
+            for o in range(planes):
+                hid_copy(a, j, o).wait_send()
+            for o in range(1, planes):
+                hid_relay(a, j, o).wait_send()
+
+        return carry
+
+    lax.fori_loop(0, n, drain, 0)
 
 
 def per_device(tokens, tangents, cotangents, routes, gates, w_up, w_down, v_up):
@@ -463,16 +504,10 @@
             pltpu.VMEM((width, hidden), BF16),
             pltpu.VMEM((hidden, width), BF16),
             pltpu.VMEM((width, hidden), BF16),
-            pltpu.VMEM((replicas,) + up, F32),
-            pltpu.VMEM((replicas,) + down, F32),
-            pltpu.VMEM((planes,) + up, BF16),
-            pltpu.VMEM((planes,) + down, BF16),
-            pltpu.VMEM((planes,) + up, BF16),
-            pltpu.VMEM((planes,) + down, BF16),
-            pltpu.VMEM((planes - 1,) + up, BF16),
-            pltpu.VMEM((planes - 1,) + down, BF16),
-            pltpu.VMEM((planes - 1,) + up, BF16),
-            pltpu.VMEM((planes - 1,) + down, BF16),
+            pltpu.VMEM(up, F32),
+            pltpu.VMEM(down, F32),
+            pltpu.VMEM((n, 3, replicas - 1, count, part), BF16),
+            pltpu.VMEM((n, 3, replicas - 1, count, hidden), BF16),
             dma((7,)),
             dma((4, 2)),
             dma((4, n)),
@@ -483,10 +518,10 @@
             dma((n, inner - 1)),
             dma((n,)),
             dma((n,)),
-            dma((2, planes)),
-            dma((2, planes)),
-            dma((2, planes - 1)),
-            dma((2, planes - 1)),
+            dma((3, n, replicas - 1)),
+            dma((3, n, replicas - 1)),
+            dma((3, n, replicas - 1)),
+            dma((3, n, replicas - 1)),
         ],
         compiler_params=pltpu.CompilerParams(
             collective_id=0, has_side_effects=True, vmem_limit_bytes=61 * 1024 * 1024

time: 168 us -> 191 us (1.14)
  Pallas kernels: 159 us -> 182 us
    pallas_call x1, Pallas kernels: 159 us -> 182 us  [per_device(): pl.pallas_call(functools.partial(layer_kernel, n, inner, cap, planes, sca...]
where the time goes in v3:
time: 191 us
  Pallas kernels  182 us (95%)
  local copies, waits for them, and re-layouts  5.05 us (3%)
  other arithmetic  2.84 us (1%)
    pallas_call x1, Pallas kernels, per_device(): pl.pallas_call(functools.partial(layer_kernel, n, inner, cap, planes, sca...  182 us
    unnamed x5, local copies, waits for them, and re-layouts  4.9 us

profile of v3, /device:TPU:0, one launch (start us, length us, event | category | flops | bytes accessed | tf_op | source)
XLA Modules:
  0.0 190.8 jit_solution(15678215276882994187)
XLA Ops:
  0.6 0.7 fusion
  1.3 0.7 convert_element_type.16
  2.0 0.7 select_reduce_fusion
  2.7 0.1 copy.15
  2.8 0.2 reduce_window_sum.11
  3.0 0.6 pad_maximum_fusion.meta
  3.6 182.3 %shard_map.103 = (bf16[128,2048]{1,0:T(8,128)(2,1)}, bf16[512,768]{1,0:T(8,128)(2,1)}, bf16[768,512]{1,0:T(8,128)(2,1)}) custom-call(f32[16,128]{1,0:T(8,128)} %pad_maximum_fusion.meta, bf16[128,2048]{1,0:T(8,128)(2,1)} %tok.1, bf16[128,2048]{1,0:T(8,128)(2,1)} %tan.1, bf16[128,2048]{1,0:T(8,128)(2,1)} %cot.1, bf16[2048,768]{1,0:T(8,128)(2,1)} %bitcast.11, ...), custom_call_target="tpu_custom_call" | custom-call | flops 14495514624 | bytes 20000000 | tf_op jit(solution)/shard_map/pallas_call | solution.py:487
  185.9 0.0 copy-start
  185.9 2.0 %copy.20 = bf16[128,2048]{1,0:T(8,128)(2,1)} copy(bf16[128,2048]{1,0:T(8,128)(2,1)} %get-tuple-element.12) | data formatting | bytes 1048576
  187.9 2.1 %copy.21 = bf16[1,512,768]{2,1,0:T(8,128)(2,1)} copy(bf16[1,512,768]{2,1,0:T(8,128)(2,1)} %bitcast.9) | data formatting | bytes 1572864
  189.9 0.0 copy-done
  190.0 0.9 copy.22
  (3 shorter events, 0.1 us)
Async XLA Ops:
  185.9 4.0 %copy-start = (bf16[768,512]{1,0:T(8,128)(2,1)S(1)}, bf16[768,512]{1,0:T(8,128)(2,1)}, u32[]{:S(2)}) copy-start(bf16[768,512]{1,0:T(8,128)(2,1)} %get-tuple-element.8) | copy-start | bytes 2359300

commit v4 on v2

--- a/solution.py
+++ b/solution.py
@@ -42,6 +42,7 @@
     y = rep // 2
     core = rep % 2
     part = acc_up.shape[1]
+    count = inner * cap
 
     def at(outer_pos, inner_pos):
         return {"expert": outer_pos * inner + inner_pos}
@@ -203,34 +204,31 @@
             device_id_type=MESH,
         )
 
-    def bring(k):
-        j = source(k)
+    def take(a, j):
         forward_left = jnp.logical_and(j > z, has_left)
         forward_right = jnp.logical_and(j < z, has_right)
 
-        def take(a):
-            @pl.when(j != z)
+        @pl.when(j != z)
+        def _():
+            hop(a, j, z, fwd_send.at[a, j]).wait_recv()
+
+            @pl.when(forward_left)
             def _():
-                hop(a, j, z, fwd_send.at[a, j]).wait_recv()
-
-                @pl.when(forward_left)
-                def _():
-                    hop(a, j, z - 1, fwd_send.at[a, j]).start()
-
-                @pl.when(forward_right)
-                def _():
-                    hop(a, j, z + 1, fwd_send.at[a, j]).start()
-
-        take(0)
-        ones, gated = picks(j)
-        for a in range(3):
-            take(a + 1)
-            pick = (gated if a == 2 else ones).astype(BF16)
-            got = jnp.dot(pick, gbuf[a, j], preferred_element_type=F32).astype(BF16)
-            rows[j, a, pl.ds(0, cap)] = got[:cap]
-            for o in range(1, inner):
-                sbuf[j, a, o - 1] = got[o * cap : (o + 1) * cap]
-                x_copy(a, j, o).start()
+                hop(a, j, z - 1, fwd_send.at[a, j]).start()
+
+            @pl.when(forward_right)
+            def _():
+                hop(a, j, z + 1, fwd_send.at[a, j]).start()
+
+    def paired(k):
+        return jnp.logical_and(k % 2 == 1, k < 2 * near)
+
+    def pass_on(a, j, pick):
+        got = jnp.dot(pick.astype(BF16), gbuf[a, j], preferred_element_type=F32).astype(BF16)
+        for o in range(1, inner):
+            sbuf[j, a, o - 1] = got[o * cap : (o + 1) * cap]
+            x_copy(a, j, o).start()
+        rows[j, a, pl.ds(0, cap)] = got[:cap]
 
     def nt(a, b):
         return lax.dot_general(a, b, (((1,), (1,)), ((), ())), preferred_element_type=F32)
@@ -305,12 +303,56 @@
                 else:
                     accs[half][c] = mine
 
-    def work(k):
+    def landed(a, j):
+        for o in range(1, inner):
+            x_arrival(a, j, o).wait_recv()
+
+    inside = jnp.logical_and(has_left, has_right)
+
+    def pass_cotangents(j):
+        _, gated = picks(j)
+        pass_on(2, j, gated)
+
+    def first_part(k):
         j = source(k)
-        for a in range(3):
-            for o in range(1, inner):
-                x_arrival(a, j, o).wait_recv()
-        count = inner * cap
+        early = jnp.logical_and(k > 0, paired(k - 1))
+
+        @pl.when(jnp.logical_not(early))
+        def _():
+            take(0, j)
+
+        ones, _ = picks(j)
+        for a in range(2):
+
+            @pl.when(jnp.logical_not(early))
+            def _():
+                take(a + 1, j)
+
+            pass_on(a, j, ones)
+
+        @pl.when(inside)
+        def _():
+            @pl.when(jnp.logical_not(early))
+            def _():
+                take(3, j)
+
+            pass_cotangents(j)
+
+            @pl.when(paired(k))
+            def _():
+                for a in range(4):
+                    take(a, source(k + 1))
+
+    def second_part(k):
+        j = source(k)
+
+        @pl.when(k == 0)
+        def _():
+            own[4].wait()
+            own[5].wait()
+
+        landed(0, j)
+        landed(1, j)
         both = rows[j, pl.ds(0, 2)].reshape(2 * count, rows.shape[3])
         up = jnp.dot(both, wu[...], preferred_element_type=F32)
         act = up[:count]
@@ -318,27 +360,33 @@
         s = 1.0 / (1.0 + jnp.exp(-act))
         s1 = s * (1.0 + act * (1.0 - s))
         s2 = s * (1.0 - s) * (2.0 + act * (1.0 - 2.0 * s))
+        s2_tan = s2 * act_tan
+        hid[j, 2] = (s1 * act_tan).astype(BF16)
+
+        @pl.when(jnp.logical_not(inside))
+        def _():
+            take(3, j)
+            pass_cotangents(j)
+
+        @pl.when(k == 0)
+        def _():
+            own[6].wait()
+
+        landed(2, j)
         back = nt(rows[j, 2], wd[...])
-        gz = (back * s1).astype(BF16)
-        gzd = (back * s2 * act_tan).astype(BF16)
-        hid[j, 0] = gzd
-        hid[j, 1] = gz
-        hid[j, 2] = (s1 * act_tan).astype(BF16)
+        hid[j, 1] = (back * s1).astype(BF16)
+        hid[j, 0] = (back * s2_tan).astype(BF16)
 
         @pl.when(k == n - 1)
         def _():
             share(j)
 
-        ha = (nt(gzd, wu[...]) + nt(gz, vu[...])).astype(BF16)
-        hback[j, pl.ds(0, cap)] = ha[:cap]
+        ha = (nt(hid[j, 0], wu[...]) + nt(hid[j, 1], vu[...])).astype(BF16)
         for o in range(1, inner):
             x_copy(0, j, o).wait_send()
             sbuf[j, 0, o - 1] = ha[o * cap : (o + 1) * cap]
             h_copy(j, o).start()
-
-        @pl.when(k < n - 1)
-        def _():
-            lax.fori_loop(0, 2 * planes, functools.partial(gather_part, j), 0)
+        hback[j, pl.ds(0, cap)] = ha[:cap]
 
     def sent(a, j):
         @pl.when(jnp.logical_and(j == z, has_left))
@@ -357,8 +405,7 @@
         def _():
             hop(a, j, z, fwd_send.at[a, j]).wait_send()
 
-    def give(k):
-        j = source(k)
+    def give(j):
         for o in range(1, inner):
             h_arrival(j, o).wait_recv()
         ones, _ = picks(j)
@@ -374,20 +421,22 @@
     def step(k, carry):
         @pl.when(k < n)
         def _():
-            bring(k)
-
-        @pl.when(k == 1)
-        def _():
-            for c in own[4:]:
-                c.wait()
-
-        @pl.when(jnp.logical_and(k >= 1, k < n + 1))
-        def _():
-            work(k - 1)
-
-        @pl.when(k >= 2)
-        def _():
-            give(k - 2)
+            first_part(k)
+
+        at_work = jnp.where(inside, k - 1, k)
+
+        @pl.when(jnp.logical_and(at_work >= 1, at_work <= n))
+        def _():
+            j = source(at_work - 1)
+            give(j)
+
+            @pl.when(at_work < n)
+            def _():
+                lax.fori_loop(0, 2 * planes, functools.partial(gather_part, j), 0)
+
+        @pl.when(jnp.logical_and(at_work >= 0, at_work < n))
+        def _():
+            second_part(at_work)
 
         return carry
 

time: 168 us -> 165 us (0.982)
  Pallas kernels: 159 us -> 156 us
    pallas_call x1, Pallas kernels: 159 us -> 156 us  [per_device(): pl.pallas_call(functools.partial(layer_kernel, n, inner, cap, planes, sca...]
where the time goes in v4:
time: 165 us
  Pallas kernels  156 us (95%)
  local copies, waits for them, and re-layouts  5.05 us (3%)
  other arithmetic  2.84 us (2%)
    pallas_call x1, Pallas kernels, per_device(): pl.pallas_call(functools.partial(layer_kernel, n, inner, cap, planes, sca...  156 us
    unnamed x5, local copies, waits for them, and re-layouts  4.9 us

profile of v4, /device:TPU:0, one launch (start us, length us, event | category | flops | bytes accessed | tf_op | source)
XLA Modules:
  0.0 164.8 jit_solution(1767280007900425188)
XLA Ops:
  0.6 0.7 fusion
  1.3 0.7 convert_element_type.16
  2.0 0.7 select_reduce_fusion
  2.7 0.1 copy.15
  2.8 0.2 reduce_window_sum.11
  3.0 0.6 pad_maximum_fusion.meta
  3.6 156.2 %shard_map.103 = (bf16[128,2048]{1,0:T(8,128)(2,1)}, bf16[512,768]{1,0:T(8,128)(2,1)}, bf16[768,512]{1,0:T(8,128)(2,1)}) custom-call(f32[16,128]{1,0:T(8,128)} %pad_maximum_fusion.meta, bf16[128,2048]{1,0:T(8,128)(2,1)} %tok.1, bf16[128,2048]{1,0:T(8,128)(2,1)} %tan.1, bf16[128,2048]{1,0:T(8,128)(2,1)} %cot.1, bf16[2048,768]{1,0:T(8,128)(2,1)} %bitcast.11, ...), custom_call_target="tpu_custom_call" | custom-call | flops 14495514624 | bytes 20000000 | tf_op jit(solution)/shard_map/pallas_call | solution.py:495
  159.9 0.0 copy-start
  159.9 2.0 %copy.20 = bf16[128,2048]{1,0:T(8,128)(2,1)} copy(bf16[128,2048]{1,0:T(8,128)(2,1)} %get-tuple-element.12) | data formatting | bytes 1048576
  161.8 2.1 %copy.21 = bf16[1,512,768]{2,1,0:T(8,128)(2,1)} copy(bf16[1,512,768]{2,1,0:T(8,128)(2,1)} %bitcast.9) | data formatting | bytes 1572864
  163.9 0.0 copy-done
  163.9 0.9 copy.22
  (3 shorter events, 0.1 us)
Async XLA Ops:
  159.9 4.0 %copy-start = (bf16[768,512]{1,0:T(8,128)(2,1)S(1)}, bf16[768,512]{1,0:T(8,128)(2,1)}, u32[]{:S(2)}) copy-start(bf16[768,512]{1,0:T(8,128)(2,1)} %get-tuple-element.8) | copy-start | bytes 2359300
